TPU v7x, 256 devices: a whole 4x4x8 slice. The times are simulated.
256 devices in a mesh: row: 32 (over x, z_hi, core), col: 8 (over y, z_lo).
Axes of the slice: x: 4, y: 4, z: 8 (z_hi: 4, z_lo: 2; z = z_hi * 2 + z_lo), core: 2. Of those that a mesh axis runs over, the one named last changes fastest.
Arguments:
- logits: float32 [8, 4096, 4096], P(None, 'row', 'col'), may hold values from -10 to 303
- values: bfloat16 [8, 4096, 256], P(None, ('col', 'row')), may hold values from -6 to 6
- output_gradient: bfloat16 [8, 4096, 256], P(None, ('col', 'row')), may hold values from -6 to 6
Outputs:
- logit_grad: float32 [8, 4096, 4096], P(None, 'row', 'col')
- value_gradient: bfloat16 [8, 4096, 256], P(None, ('col', 'row'))
All inputs are finite; a program needn't handle non-finite values.
Results may differ from a plain program's by a relative error of at most 0.0049.
Values may be sent and summed in bfloat16 or wider, within the bound.
A program may use at most 64 MiB of HBM per device.

v0:
```python
import jax
import jax.numpy as jnp
from jax import lax
from jax.sharding import PartitionSpec as P


def broadcast(value, axis, source):
    kept = jnp.where(lax.axis_index(axis) == source, value, 0).astype(value.dtype)
    return lax.psum(kept, axis)


def per_device(logits, values, output_gradient):
    head_total, query_total, key_total = logits.shape
    alignment_rows, own_total, feature_total = values.shape
    channel_total = feature_total // head_total
    group_rows = lax.axis_size("row") // lax.axis_size("col")
    row_id = lax.axis_index("row")
    value_key_rows, grad_keys = (
        lax.all_gather(values, "row", axis=1, tiled=True),
        lax.all_gather(output_gradient, "row", axis=1, tiled=True),
    )
    offset = row_id % group_rows * query_total
    own_rows = lax.dynamic_slice_in_dim(grad_keys, offset, query_total, 1)
    query_gradient = broadcast(own_rows, "col", row_id // group_rows)
    local_max = jnp.max(logits, axis=2)
    row_max = lax.pmax(local_max, "col")
    exponent = jnp.exp(logits - row_max[:, :, None])
    total = lax.psum(jnp.sum(exponent, axis=2), "col")
    weights = exponent / total[:, :, None]
    query_head_split = query_gradient.reshape(
        alignment_rows, query_total, head_total, channel_total
    )
    key_head_split = value_key_rows.reshape(alignment_rows, key_total, head_total, channel_total)
    weight_grad = jnp.einsum(
        "sihc,sjhc->hij", query_head_split, key_head_split, preferred_element_type=jnp.float32
    )
    row_dot = lax.psum(jnp.sum(weights * weight_grad, axis=2), "col")
    logit_grad = weights * (weight_grad - row_dot[:, :, None])
    weights_half = weights.astype(jnp.bfloat16)
    addend_piece = jnp.einsum(
        "hij,sihc->sjhc", weights_half, query_head_split, preferred_element_type=jnp.float32
    )
    reduced_total = lax.psum(addend_piece.reshape(alignment_rows, key_total, feature_total), "row")
    value_gradient = lax.dynamic_slice_in_dim(reduced_total, row_id * own_total, own_total, 1)
    return (logit_grad, value_gradient.astype(jnp.bfloat16))


def solution(mesh):
    placed = (P(None, "row", "col"), P(None, ("col", "row"), None), P(None, ("col", "row"), None))
    return jax.shard_map(
        per_device,
        mesh=mesh,
        in_specs=placed,
        out_specs=(P(None, "row", "col"), P(None, ("col", "row"), None)),
        check_vma=False,
    )
```

profile of v0, /device:TPU:1, one launch (start us, length us, event | category | flops | bytes accessed | tf_op | source)
XLA Modules:
  0.0 409.2 jit_solution(16823460712732998251)
XLA Ops:
  7.2 0.0 all-gather.3.cloned.1.call-start
  7.2 1.5 copy.11
  8.7 0.0 all-gather.3.cloned.1.call-update
  8.7 0.0 all-gather.5.cloned.1.call-start
  8.8 1.5 copy.14
  10.3 0.0 all-gather.5.cloned.1.call-update
  10.3 0.0 all-reduce.3.cloned.1.call-start
  10.4 59.7 %all-gather.3.cloned.1.call-done = bf16[8,512,256]{2,0,1:T(8,128)(2,1)} async-done(((bf16[8,16,256]{2,0,1:T(8,128)(2,1)}), bf16[8,512,256]{2,0,1:T(8,128)(2,1)}) %all-gather.3.cloned.1.call-update) | async-done | bytes 2097168 | tf_op jit(solution)/shard_map/all_gather | solution.py:20
  70.1 1.1 constant_dynamic-slice_fusion
  71.1 0.0 copy-start
  71.2 0.4 copy.21
  71.6 0.8 copy.13
  72.5 0.0 all-reduce.3.cloned.1.call-update
  72.5 0.4 copy-done
  72.9 0.2 reduce_max.9
  73.1 14.3 %pmax.7 = f32[8,128]{1,0:T(8,128)S(1)} all-reduce(f32[8,128]{1,0:T(8,128)S(1)} %reduce_max.9), channel_id=1, replica_groups=mesh['row'=32,'col'=8] {'col'}, use_global_device_ids=true, to_apply=%region_1.2 | all-reduce | flops 1024 | bytes 8192 | tf_op jit(solution)/shard_map/pmax | solution.py:26
  87.5 0.6 fusion.5
  88.1 12.9 %psum.28 = f32[8,128]{1,0:T(8,128)S(1)} all-reduce(f32[8,128]{1,0:T(8,128)S(1)} %fusion.5), channel_id=1, replica_groups=mesh['row'=32,'col'=8] {'col'}, use_global_device_ids=true, to_apply=%region_3.4 | all-reduce | flops 1024 | bytes 8192 | tf_op jit(solution)/shard_map/psum | solution.py:28
  101.0 23.8 %all-gather.5.cloned.1.call-done = bf16[8,512,256]{2,0,1:T(8,128)(2,1)} async-done(((bf16[8,16,256]{2,0,1:T(8,128)(2,1)}), bf16[8,512,256]{2,0,1:T(8,128)(2,1)}) %all-gather.5.cloned.1.call-update) | async-done | bytes 2097168 | tf_op jit(solution)/shard_map/all_gather | solution.py:19
  124.8 4.3 %copy.15 = bf16[8,512,256]{1,2,0:T(8,128)(2,1)} copy(bf16[8,512,256]{2,0,1:T(8,128)(2,1)} %all-gather.5.cloned.1.call-done) | data formatting | bytes 4194304 | tf_op jit(solution)/shard_map/all_gather | solution.py:19
  129.1 70.7 %all-reduce.3.cloned.1.call-done = bf16[8,128,8,32]{1,3,0,2:T(8,128)(2,1)} async-done(((bf16[8,128,8,32]{1,3,0,2:T(8,128)(2,1)}), bf16[8,128,8,32]{1,3,0,2:T(8,128)(2,1)}) %all-reduce.3.cloned.1.call-update) | async-done | bytes 524304 | tf_op jit(solution)/shard_map/psum | solution.py:9
  199.8 1.9 convolution_bitcast_fusion
  201.7 2.4 copy.17
  204.1 0.0 copy-start.1
  204.1 175.1 %all-reduce.4 = bf16[8,512,256]{1,2,0:T(8,128)(2,1)} all-reduce(f32[8,512,256]{1,2,0:T(8,128)} %bitcast.20), channel_id=1, replica_groups=mesh['row'=32,'col'=8] {'row'}, use_global_device_ids=true, to_apply=%region_7.8 | all-reduce | flops 1048576 | bytes 6291456 | tf_op jit(solution)/shard_map/psum | solution.py:43
  379.3 1.2 dynamic-slice_convert_fusion
  380.5 0.8 copy.18
  381.3 0.0 copy-done.1
  381.3 3.5 fusion
  384.9 14.4 %psum.30 = f32[8,128]{1,0:T(8,128)S(1)} all-reduce(f32[8,128]{1,0:T(8,128)S(1)} %get-tuple-element.6), channel_id=1, replica_groups=mesh['row'=32,'col'=8] {'col'}, use_global_device_ids=true, to_apply=%region_6.7 | all-reduce | flops 1024 | bytes 8192 | tf_op jit(solution)/shard_map/psum | solution.py:37
  399.3 3.4 fusion.1
  (1 shorter events, 0.0 us)
Async XLA Ops:
  7.2 62.9 %all-gather.3.cloned.1.call-start = ((), (), s32[]{:S(2)}) async-start(), calls=%async_computation | async-start | bytes 2162688 | tf_op jit(solution)/shard_map/all_gather | solution.py:20
  8.7 116.1 %all-gather.5.cloned.1.call-start = ((), (), s32[]{:S(2)}) async-start(), calls=%async_computation.2 | async-start | bytes 2162688 | tf_op jit(solution)/shard_map/all_gather | solution.py:19
  10.3 189.5 %all-reduce.3.cloned.1.call-start = ((), (), s32[]{:S(2)}) async-start(), calls=%async_computation.1 | async-start | bytes 1048576 | tf_op jit(solution)/shard_map/psum | solution.py:9
  71.1 1.8 copy-start
  204.1 177.2 %copy-start.1 = (bf16[8,128,8,32]{1,3,0,2:T(8,128)(2,1)S(1)}, bf16[8,128,8,32]{1,3,0,2:T(8,128)(2,1)}, u32[]{:S(2)}) copy-start(bf16[8,128,8,32]{1,3,0,2:T(8,128)(2,1)} %all-reduce.3.cloned.1.call-done) | copy-start | bytes 1572868
Sparse Core Ops, SparseCore 0:
  11.1 58.8 all-gather.2
  73.2 51.5 all-gather.4
  127.5 72.3 all-reduce.2
where the time goes:
time: 416 us; the launch traced here: 409 us
  blocking collectives  217 us (52%)
  waiting for transfers between devices  154 us (37%)
  local copies, waits for them, and re-layouts  14.5 us (3%)
  between operations  13.8 us (3%)
  matrix products  5.4 us (1%)
  other arithmetic  4.31 us (1%)
    psum x1, blocking collectives, per_device(): lax.psum(addend_piece.reshape(alignment_rows, key_total, feature_total),...  175 us
    psum x1, waiting for transfers between devices, broadcast(): return lax.psum(kept, axis)  70.7 us
    all_gather x1, waiting for transfers between devices, per_device(): lax.all_gather(output_gradient, 'row', axis=1, tiled=True)  59.7 us
    all_gather x1, waiting for transfers between devices, per_device(): lax.all_gather(values, 'row', axis=1, tiled=True)  23.8 us
    psum x1, blocking collectives, per_device(): row_dot = lax.psum(jnp.sum(weights * weight_grad, axis=2), 'col')  14.4 us
    pmax x1, blocking collectives, per_device(): row_max = lax.pmax(local_max, 'col')  14.3 us
    psum x1, blocking collectives, per_device(): total = lax.psum(jnp.sum(exponent, axis=2), 'col')  12.9 us
  transfers between devices with their start and end apart: 3, of which 3 were waited for; matrix products, arithmetic and copies ran while one was open for 2% of the time, Pallas kernels for 0%

commit v1 on v0

v1 whole, which is shorter than its diff:
```python
import functools

import jax
import jax.numpy as jnp
from jax import lax
from jax.experimental import pallas as pl
from jax.experimental.pallas import tpu as pltpu
from jax.sharding import PartitionSpec as P

RING = 4
HEADS = 8
BLOCK = 16
F32 = jnp.float32
BF16 = jnp.bfloat16


def regroup(pieces, width):
    count = pieces[0].shape[1] // width
    return [
        jnp.concatenate([piece[:, b * width : (b + 1) * width] for piece in pieces], axis=1)
        for b in range(count)
    ]


def kernel(
    logits_ref, values_ref, grads_ref, logit_grad_ref, value_grad_ref,
    vals, ogs, own_grads, wts, wgs, part, core_in, xhalf, xfull, zhalf, zfull,
    stat, dots, load_sem, store_sem, send_sem, recv_sem,
):
    row, col = lax.axis_index("row"), lax.axis_index("col")
    x, zh, k = row // 8, row // 2 % 4, row % 2
    y, zl = col // 2, col % 2

    def at(x=x, zh=zh, k=k, y=y, zl=zl):
        return {"row": (x % 4) * 8 + (zh % 4) * 2 + k, "col": (y % 4) * 2 + zl}

    def slot(dx=0, dz=0):
        return (x + dx + 4) % 4 * 4 + (zh + dz + 4) % 4

    def line(dx=0, dz=0, core=k):
        return slot(dx, dz) * 2 + core

    started = []

    def send(src, dst, where):
        n = len(started)
        copy = pltpu.make_async_remote_copy(
            src_ref=src, dst_ref=dst, send_sem=send_sem.at[n], recv_sem=recv_sem.at[n],
            device_id=where, device_id_type=pl.DeviceIdType.MESH,
        )
        copy.start()
        started.append(copy)
        return copy

    sibling = at(k=1 - k)
    xs = {1: at(x=x + 1), -1: at(x=x + 3)}
    zs = {1: at(zh=zh + 1), -1: at(zh=zh + 3)}
    ys = {1: at(y=y + 1), -1: at(y=y + 3)}
    cols = [{"row": row, "col": (col + d) % 8} for d in range(1, 8)]
    grads_from = at(x=zh % 2 * 2 + k, zh=y + 2, k=zl, y=x, zl=zh // 2)
    grads_to = at(x=y, zh=zl * 2 + x // 2, k=x % 2, y=zh + 2, zl=k)

    loads = []
    for h in range(HEADS):
        load = pltpu.make_async_copy(logits_ref.at[h], wts.at[h], load_sem.at[h])
        load.start()
        loads.append(load)

    barrier = pltpu.get_barrier_semaphore()
    greeted = [sibling, *xs.values(), *zs.values(), *cols, grads_from]
    for device in greeted:
        pl.semaphore_signal(barrier, inc=1, device_id=device, device_id_type=pl.DeviceIdType.MESH)

    for h, piece in enumerate(regroup([grads_ref[s] for s in range(8)], 32)):
        own_grads[h] = piece
    for h, piece in enumerate(regroup([values_ref[s] for s in range(8)], 32)):
        vals[row, h] = piece

    pl.semaphore_wait(barrier, len(greeted))

    piece = zh * 2 + k
    grads_in = send(own_grads, ogs.at[piece], grads_to)

    def share(ref_slot, where, heads=None):
        ref = vals.at[ref_slot] if heads is None else vals.at[ref_slot, pl.ds(heads, 4)]
        return send(ref, ref, where)

    z_first = {d: share(row, zs[d]) for d in (1, -1)}
    x_first = {0: {d: share(row, xs[d]) for d in (1, -1)}}
    core_values = [share(row, sibling)]

    lanes = lax.broadcasted_iota(jnp.int32, (128, 128), 1)
    table = jnp.zeros((128, 128), F32)
    for h in range(HEADS):
        loads[h].wait()
        block = wts[h]
        top = jnp.max(block, axis=1, keepdims=True)
        exponent = jnp.exp(block - top)
        wts[h] = exponent
        table = jnp.where(lanes == h, top, table)
        table = jnp.where(lanes == 8 + h, jnp.sum(exponent, axis=1, keepdims=True), table)
    stat[col] = table.T[:16]
    stat_in = [send(stat.at[col], stat.at[col], device) for device in cols]

    grads_in.wait_recv()
    mine = (col + 4) % 8
    other = (at(zl=1 - zl)["col"] + 4) % 8
    twin_in = send(ogs.at[mine], ogs.at[mine], at(zl=1 - zl))
    y_own = {d: send(ogs.at[mine], ogs.at[mine], ys[d]) for d in (1, -1)}

    def of_y(p, d):
        return (p - 2 * d + 8) % 8

    z_second = {}
    for d in (1, -1):
        z_first[d].wait_recv()
        got = line(dz=-d)
        z_second[d] = share(got, zs[d], 0 if d == 1 else 4)
        x_first[-d] = {e: share(got, xs[e]) for e in (1, -1)}
        core_values.append(share(got, sibling))

    twin_in.wait_recv()
    y_other = {d: send(ogs.at[other], ogs.at[other], ys[d]) for d in (1, -1)}

    x_second = []

    def x_arrivals(dz):
        for d in (1, -1):
            x_first[dz][d].wait_recv()
            got = line(dx=-d, dz=dz)
            x_second.append(share(got, xs[d], 0 if d == 1 else 4))
            core_values.append(share(got, sibling))

    x_arrivals(0)

    y_own[1].wait_recv()
    got = of_y(mine, 1)
    y_second_a = send(ogs.at[got], ogs.at[got], ys[1])
    y_own[-1].wait_recv()

    for copy in z_second.values():
        copy.wait_recv()
    got = line(dz=2)
    x_first[2] = {e: share(got, xs[e]) for e in (1, -1)}
    core_values.append(share(got, sibling))

    y_other[-1].wait_recv()
    got = of_y(other, -1)
    y_second_b = send(ogs.at[got], ogs.at[got], ys[-1])
    y_other[1].wait_recv()

    for copy in stat_in:
        copy.wait_recv()
    tops, sums = stat[:, 0:8, :], stat[:, 8:16, :]
    top = jnp.max(tops, axis=0)
    total = jnp.sum(sums * jnp.exp(tops - top[None]), axis=0)
    factor = jnp.exp(stat[col, 0:8, :] - top) / total
    factor = jnp.concatenate([factor] * 16, axis=0).T

    x_arrivals(-1)
    x_arrivals(1)

    y_second_a.wait_recv()
    y_second_b.wait_recv()

    core_sums = []
    for h in range(HEADS):
        weight = wts[h] * factor[:, h : h + 1]
        wts[h] = weight
        og = ogs[:, h].reshape(128, 256)
        addend = lax.dot_general(
            weight.astype(BF16), og, (((0,), (0,)), ((), ())), preferred_element_type=F32
        ).astype(BF16).reshape(16, 2, BLOCK, 256)
        part[0, h] = addend[:, 0]
        part[1, h] = addend[:, 1]
        core_sums.append(send(part.at[1 - k, h], core_in.at[h], sibling))

    x_arrivals(2)

    for copy in core_sums:
        copy.wait_recv()

    def add_core(s):
        part[k, :, s] = (part[k, :, s].astype(F32) + core_in[:, s].astype(F32)).astype(BF16)

    order = (2, 1, -1, 0)
    half_in = {}
    for dz in order:
        s = slot(2, dz)
        add_core(s)
        for d in (1, -1):
            heads = pl.ds(0 if d == 1 else 4, 4)
            half_in[dz, d] = send(part.at[k, heads, s], xhalf.at[0 if d == 1 else 1, :, slot(0, dz) % 4], xs[d])

    for copy in x_second:
        copy.wait_recv()
    for dz in (0, -1, 1, 2):
        core_values.append(share(line(dx=2, dz=dz), sibling))

    full_in = {}
    for dz in order:
        for d in (1, -1):
            s = slot(d, dz)
            add_core(s)
            half_in[dz, d].wait_recv()
            heads = pl.ds(0 if d == 1 else 4, 4)
            part[k, heads, s] = (
                part[k, heads, s].astype(F32) + xhalf[0 if d == 1 else 1, :, slot(0, dz) % 4].astype(F32)
            ).astype(BF16)
            full_in[dz, d] = send(part.at[k, :, s], xfull.at[0 if d == 1 else 1, :, slot(0, dz) % 4], xs[d])
    for dz in order:
        add_core(slot(0, dz))

    for copy in core_values:
        copy.wait_recv()
    table = jnp.zeros((128, 128), F32)
    for h in range(HEADS):
        weight_grad = lax.dot_general(
            ogs[:, h].reshape(128, 256), vals[:, h].reshape(512, 256),
            (((1,), (1,)), ((), ())), preferred_element_type=F32,
        )
        wgs[h] = weight_grad
        table = jnp.where(lanes == h, jnp.sum(weight_grad * wts[h], axis=1, keepdims=True), table)
    dots[col] = table.T[:8]
    dot_in = [send(dots.at[col], dots.at[col], device) for device in cols]

    def arrived(dz):
        s = slot(0, dz)
        total = part[k, :, s].astype(F32)
        for d in (1, -1):
            full_in[dz, d].wait_recv()
            total += xfull[0 if d == 1 else 1, :, slot(0, dz) % 4].astype(F32)
        return s, total

    s, total = arrived(2)
    part[k, :, s] = total.astype(BF16)
    z_half = {}
    for d in (1, -1):
        heads = pl.ds(0 if d == 1 else 4, 4)
        z_half[d] = send(part.at[k, heads, s], zhalf.at[0 if d == 1 else 1], zs[d])

    for copy in dot_in:
        copy.wait_recv()
    row_dot = jnp.sum(dots[...], axis=0)
    row_dot = jnp.concatenate([row_dot] * 16, axis=0).T
    stores = []
    for h in range(HEADS):
        wgs[h] = wts[h] * (wgs[h] - row_dot[:, h : h + 1])
        store = pltpu.make_async_copy(wgs.at[h], logit_grad_ref.at[h], store_sem.at[h])
        store.start()
        stores.append(store)

    z_full = {}
    for d in (1, -1):
        s, total = arrived(d)
        z_half[d].wait_recv()
        if d == 1:
            part[k, 0:4, s] = (total[0:4] + zhalf[0].astype(F32)).astype(BF16)
            part[k, 4:8, s] = total[4:8].astype(BF16)
        else:
            part[k, 0:4, s] = total[0:4].astype(BF16)
            part[k, 4:8, s] = (total[4:8] + zhalf[1].astype(F32)).astype(BF16)
        z_full[d] = send(part.at[k, :, s], zfull.at[0 if d == 1 else 1], zs[d])
    s, total = arrived(0)
    for d in (1, -1):
        z_full[d].wait_recv()
        total += zfull[0 if d == 1 else 1].astype(F32)
    for s, piece in enumerate(regroup([total[h] for h in range(8)], 32)):
        value_grad_ref[s] = piece.astype(BF16)

    for store in stores:
        store.wait()
    for copy in started:
        copy.wait_send()


def per_device(logits, values, output_gradient):
    vmem = pl.BlockSpec(memory_space=pltpu.VMEM)
    hbm = pl.BlockSpec(memory_space=pl.ANY)
    copies = 112
    return pl.pallas_call(
        kernel,
        out_shape=(
            jax.ShapeDtypeStruct(logits.shape, F32),
            jax.ShapeDtypeStruct(values.shape, BF16),
        ),
        in_specs=[hbm, vmem, vmem],
        out_specs=(hbm, vmem),
        scratch_shapes=[
            pltpu.VMEM((32, HEADS, BLOCK, 256), BF16),
            pltpu.VMEM((8, HEADS, BLOCK, 256), BF16),
            pltpu.VMEM((HEADS, BLOCK, 256), BF16),
            pltpu.VMEM((HEADS, 128, 512), F32),
            pltpu.VMEM((HEADS, 128, 512), F32),
            pltpu.VMEM((2, HEADS, 16, BLOCK, 256), BF16),
            pltpu.VMEM((HEADS, 16, BLOCK, 256), BF16),
            pltpu.VMEM((2, 4, RING, BLOCK, 256), BF16),
            pltpu.VMEM((2, HEADS, RING, BLOCK, 256), BF16),
            pltpu.VMEM((2, 4, BLOCK, 256), BF16),
            pltpu.VMEM((2, HEADS, BLOCK, 256), BF16),
            pltpu.VMEM((8, 16, 128), F32),
            pltpu.VMEM((8, 8, 128), F32),
            pltpu.SemaphoreType.DMA((HEADS,)),
            pltpu.SemaphoreType.DMA((HEADS,)),
            pltpu.SemaphoreType.DMA((copies,)),
            pltpu.SemaphoreType.DMA((copies,)),
        ],
        compiler_params=pltpu.CompilerParams(
            collective_id=0, has_side_effects=True, vmem_limit_bytes=40 * 1024 * 1024
        ),
    )(logits, values, output_gradient)


def solution(mesh):
    placed = (P(None, "row", "col"), P(None, ("col", "row"), None), P(None, ("col", "row"), None))
    return jax.shard_map(
        per_device,
        mesh=mesh,
        in_specs=placed,
        out_specs=(P(None, "row", "col"), P(None, ("col", "row"), None)),
        check_vma=False,
    )
```

time: 416 us -> 58.9 us (0.14); the launches traced: 409 us -> 58.7 us
  blocking collectives: 217 us -> 0 us
  waiting for transfers between devices: 154 us -> 0 us
  Pallas kernels: 0 us -> 52.9 us
  between operations: 13.8 us -> 0.65 us
  local copies, waits for them, and re-layouts: 14.5 us -> 5.21 us
  matrix products: 5.4 us -> 0 us
  other arithmetic: 4.31 us -> 0 us
    psum x3 -> x0, blocking collectives: 202 us -> none  [the longest x1 175 us: per_device(): lax.psum(addend_piece.reshape(alignment_rows, key_total, feature_total),...]
    all_gather x2 -> x0, waiting for transfers between devices: 83.5 us -> none  [the longest x1 59.7 us: per_device(): lax.all_gather(output_gradient, 'row', axis=1, tiled=True)]
    psum x1 -> x0, waiting for transfers between devices: 70.7 us -> none  [broadcast(): return lax.psum(kept, axis)]
    pallas_call x0 -> x1, Pallas kernels: none -> 52.9 us  [per_device(): pl.pallas_call(kernel, out_shape=(jax.ShapeDtypeStruct(logits.shape, F32)...]
    pmax x1 -> x0, blocking collectives: 14.3 us -> none  [per_device(): row_max = lax.pmax(local_max, 'col')]
    dot_general x2 -> x0, matrix products: 5.4 us -> none  [the longest x1 3.54 us: per_device(): jnp.einsum('sihc,sjhc->hij', query_head_split, key_head_split, preferred_...]
    all_gather x1 -> x0, local copies, waits for them, and re-layouts: 4.26 us -> none  [per_device(): lax.all_gather(values, 'row', axis=1, tiled=True)]
  transfers between devices with their start and end apart: 3 -> 0, of which waited for: 3 -> 0; matrix products, arithmetic and copies ran while one was open for 2% -> 0% of each run, Pallas kernels for 0% -> 0%
where the time goes in v1:
time: 58.9 us; the launch traced here: 58.7 us
  Pallas kernels  52.9 us (90%)
  local copies, waits for them, and re-layouts  5.21 us (9%)
  between operations  0.65 us (1%)
    pallas_call x1, Pallas kernels, per_device(): pl.pallas_call(kernel, out_shape=(jax.ShapeDtypeStruct(logits.shape, F32)...  52.9 us
    unnamed x8, local copies, waits for them, and re-layouts  5.21 us

profile of v1, /device:TPU:1, one launch (start us, length us, event | category | flops | bytes accessed | tf_op | source)
XLA Modules:
  0.0 58.7 jit_solution(9347274526517641679)
XLA Ops:
  0.6 0.0 copy-start
  0.6 1.6 %copy-done = f32[8,128,512]{2,1,0:T(8,128)S(1)} copy-done((f32[8,128,512]{2,1,0:T(8,128)S(1)}, f32[8,128,512]{2,1,0:T(8,128)}, u32[]{:S(2)}) %copy-start) | copy-done | bytes 2097176
  2.2 0.0 copy-start.1
  2.2 0.8 %copy-done.1 = bf16[8,16,256]{2,1,0:T(8,128)(2,1)S(1)} copy-done((bf16[8,16,256]{2,1,0:T(8,128)(2,1)S(1)}, bf16[8,16,256]{2,1,0:T(8,128)(2,1)}, u32[]{:S(2)}) %copy-start.1) | copy-done | bytes 65560
  3.1 0.0 copy-start.2
  3.1 0.8 %copy-done.2 = bf16[8,16,256]{2,1,0:T(8,128)(2,1)S(1)} copy-done((bf16[8,16,256]{2,1,0:T(8,128)(2,1)S(1)}, bf16[8,16,256]{2,1,0:T(8,128)(2,1)}, u32[]{:S(2)}) %copy-start.2) | copy-done | bytes 65560
  3.9 52.9 %shard_map.50 = (f32[8,128,512]{2,1,0:T(8,128)S(1)}, bf16[8,16,256]{2,1,0:T(8,128)(2,1)S(1)}) custom-call(f32[8,128,512]{2,1,0:T(8,128)S(1)} %copy-done, bf16[8,16,256]{2,1,0:T(8,128)(2,1)S(1)} %copy-done.1, bf16[8,16,256]{2,1,0:T(8,128)(2,1)S(1)} %copy-done.2), custom_call_target="tpu_custom_call" | custom-call | tf_op jit(solution)/shard_map/pallas_call | solution.py:281
  56.8 1.3 %copy.7 = f32[8,128,512]{2,1,0:T(8,128)} copy(f32[8,128,512]{2,1,0:T(8,128)S(1)} %get-tuple-element.4) | data formatting | bytes 4194304
  58.1 0.6 %copy.8 = bf16[8,16,256]{2,1,0:T(8,128)(2,1)} copy(bf16[8,16,256]{2,1,0:T(8,128)(2,1)S(1)} %get-tuple-element.5) | data formatting | bytes 131072
Async XLA Ops:
  0.6 1.6 %copy-start = (f32[8,128,512]{2,1,0:T(8,128)S(1)}, f32[8,128,512]{2,1,0:T(8,128)}, u32[]{:S(2)}) copy-start(f32[8,128,512]{2,1,0:T(8,128)} %logits_ref.1) | copy-start | bytes 6291460
  2.2 0.8 %copy-start.1 = (bf16[8,16,256]{2,1,0:T(8,128)(2,1)S(1)}, bf16[8,16,256]{2,1,0:T(8,128)(2,1)}, u32[]{:S(2)}) copy-start(bf16[8,16,256]{2,1,0:T(8,128)(2,1)} %values_ref.1) | copy-start | bytes 196612
  3.1 0.8 %copy-start.2 = (bf16[8,16,256]{2,1,0:T(8,128)(2,1)S(1)}, bf16[8,16,256]{2,1,0:T(8,128)(2,1)}, u32[]{:S(2)}) copy-start(bf16[8,16,256]{2,1,0:T(8,128)(2,1)} %grads_ref.1) | copy-start | bytes 196612

commit v2 on v1

v2 whole, which is shorter than its diff:
```python
import functools

import jax
import jax.numpy as jnp
from jax import lax
from jax.experimental import pallas as pl
from jax.experimental.pallas import tpu as pltpu
from jax.sharding import PartitionSpec as P

RING = 4
HEADS = 8
GROUP = 4
HALF = 2
BLOCK = 16
F32 = jnp.float32
BF16 = jnp.bfloat16


def regroup(pieces, width):
    count = pieces[0].shape[1] // width
    return [
        jnp.concatenate([piece[:, b * width : (b + 1) * width] for piece in pieces], axis=1)
        for b in range(count)
    ]


def kernel(
    logits_ref, values_ref, grads_ref, logit_grad_ref, value_grad_ref,
    raw, vals, ogs, own_grads, wts, wgs, part, core_in, xhalf, xfull, zfull,
    stat, dots, load_sem, send_sem, recv_sem,
):
    row, col = lax.axis_index("row"), lax.axis_index("col")
    x, zh, k = row // 8, row // 2 % 4, row % 2
    y, zl = col // 2, col % 2

    def at(x=x, zh=zh, k=k, y=y, zl=zl):
        return {"row": (x % 4) * 8 + (zh % 4) * 2 + k, "col": (y % 4) * 2 + zl}

    def slot(dx=0, dz=0):
        return (x + dx + 4) % 4 * 4 + (zh + dz + 4) % 4

    def line(dx=0, dz=0, core=k):
        return slot(dx, dz) * 2 + core

    started = []

    def send(src, dst, where):
        n = len(started)
        copy = pltpu.make_async_remote_copy(
            src_ref=src, dst_ref=dst, send_sem=send_sem.at[n], recv_sem=recv_sem.at[n],
            device_id=where, device_id_type=pl.DeviceIdType.MESH,
        )
        copy.start()
        started.append(copy)
        return copy

    sibling = at(k=1 - k)
    xs = {d: at(x=x + d + 4) for d in (1, -1)}
    zs = {d: at(zh=zh + d + 4) for d in (1, -1, 2)}
    ys = {d: at(y=y + d + 4) for d in (1, -1, 2)}
    twin = at(zl=1 - zl)
    cols = [{"row": row, "col": (col + d) % 8} for d in range(1, 8)]
    grads_to = at(x=y, zh=zl * 2 + x // 2, k=x % 2, y=zh, zl=1 - k)
    grads_from = at(x=zh % 2 * 2 + k, zh=y, k=1 - zl, y=x, zl=zh // 2)

    barrier = pltpu.get_barrier_semaphore()
    greeted = [grads_from, *zs.values(), *xs.values(), *cols, sibling]
    for device in greeted:
        pl.semaphore_signal(barrier, inc=1, device_id=device, device_id_type=pl.DeviceIdType.MESH)

    def load(src, dst, n):
        copy = pltpu.make_async_copy(src, dst, load_sem.at[n])
        copy.start()
        loads.append(copy)

    loads = []
    load(grads_ref, raw.at[0], HEADS)
    load(values_ref, raw.at[1], HEADS + 1)
    for h in range(HEADS):
        load(logits_ref.at[h], wts.at[h], h)
    loads[0].wait()
    for h, piece in enumerate(regroup([raw[0, s] for s in range(8)], 32)):
        own_grads[h] = piece
    loads[1].wait()
    for h, piece in enumerate(regroup([raw[1, s] for s in range(8)], 32)):
        vals[row, h] = piece
    loads = loads[2:]

    pl.semaphore_wait(barrier, len(greeted))

    groups = [pl.ds(h, GROUP) for h in range(0, HEADS, GROUP)]

    piece = zh * 2 + k
    grads_in = [send(own_grads.at[heads], ogs.at[piece, heads], grads_to) for heads in groups]

    def share(ref_slot, where, heads=None):
        ref = vals.at[ref_slot] if heads is None else vals.at[ref_slot, pl.ds(heads, 4)]
        return send(ref, ref, where)

    x_first = {0: {d: share(row, xs[d]) for d in (1, -1)}}
    z_first = {d: share(row, zs[d]) for d in (1, -1)}
    z_second = {}
    core_values = [share(row, sibling)]

    lanes = lax.broadcasted_iota(jnp.int32, (128, 128), 1)
    table = jnp.zeros((128, 128), F32)
    for h in range(HEADS):
        loads[h].wait()
        block = wts[h]
        top = jnp.max(block, axis=1, keepdims=True)
        exponent = jnp.exp(block - top)
        wts[h] = exponent
        table = jnp.where(lanes == h, top, table)
        table = jnp.where(lanes == 8 + h, jnp.sum(exponent, axis=1, keepdims=True), table)
    stat[col] = table.T[:16]
    stat_in = [send(stat.at[col], stat.at[col], device) for device in cols]

    mine, other = y * 2 + (1 - zl), y * 2 + zl

    def pass_on(which, heads, where):
        return send(ogs.at[which, heads], ogs.at[which, heads], where)

    twin_in, y_in = [], []
    for g, heads in enumerate(groups):
        grads_in[g].wait_recv()
        twin_in.append(pass_on(mine, heads, twin))
        y_in.append([pass_on(mine, heads, ys[d]) for d in (1, -1, 2)])

    def z_arrival(d):
        got = line(dz=-d)
        if d == 2:
            for copy in z_second.values():
                copy.wait_recv()
        else:
            z_first[d].wait_recv()
            z_second[d] = share(got, zs[d], 0 if d == 1 else 4)
        x_first[2 if d == 2 else -d] = {e: share(got, xs[e]) for e in (1, -1)}
        core_values.append(share(got, sibling))

    x_second = []

    def x_arrivals(dz):
        for d in (1, -1):
            x_first[dz][d].wait_recv()
            got = line(dx=-d, dz=dz)
            x_second.append(share(got, xs[d], 0 if d == 1 else 4))
            core_values.append(share(got, sibling))

    z_arrival(1)
    z_arrival(-1)
    x_arrivals(0)
    for g, heads in enumerate(groups):
        twin_in[g].wait_recv()
        y_in[g] += [pass_on(other, heads, ys[d]) for d in (1, -1, 2)]

    for copy in stat_in:
        copy.wait_recv()
    tops, sums = stat[:, 0:8, :], stat[:, 8:16, :]
    top = jnp.max(tops, axis=0)
    total = jnp.sum(sums * jnp.exp(tops - top[None]), axis=0)
    factor = jnp.exp(stat[col, 0:8, :] - top) / total
    factor = jnp.concatenate([factor] * 16, axis=0).T
    for h in range(HEADS):
        wts[h] = wts[h] * factor[:, h : h + 1]
    z_arrival(2)

    core_sums = []

    def addends(g):
        for copy in y_in[g]:
            copy.wait_recv()
        for h in range(g * GROUP, (g + 1) * GROUP):
            og = ogs[:, h].reshape(128, 256)
            addend = lax.dot_general(
                wts[h].astype(BF16), og, (((0,), (0,)), ((), ())), preferred_element_type=F32
            ).astype(BF16).reshape(16, 2, BLOCK, 256)
            part[0, h] = addend[:, 0]
            part[1, h] = addend[:, 1]
            if h % HALF == HALF - 1:
                heads = pl.ds(h - HALF + 1, HALF)
                core_sums.append(send(part.at[1 - k, heads], core_in.at[heads], sibling))

    order = (2, 1, -1, 0)
    place = {1: 0, -1: 1, 2: 2}

    def half_of(g, d):
        return pl.ds(g * GROUP + (0 if d == 1 else HALF), HALF)

    def zslot(dz):
        return (zh + dz + 4) % 4

    half_in, full_in = {}, {}

    def send_halves(g):
        for d in (1, -1):
            heads = half_of(g, d)
            core_sums[g * 2 + place[d]].wait_recv()
            for dz in order:
                s = slot(2, dz)
                part[k, heads, s] = (part[k, heads, s].astype(F32) + core_in[heads, s].astype(F32)).astype(BF16)
                half_in[g, dz, d] = send(part.at[k, heads, s], xhalf.at[place[d], g, :, zslot(dz)], xs[d])

    def send_fulls(g):
        for dz in order:
            for d in (1, -1):
                s = slot(d, dz)
                heads = half_of(g, -d)
                part[k, heads, s] = (part[k, heads, s].astype(F32) + core_in[heads, s].astype(F32)).astype(BF16)
                half_in[g, dz, d].wait_recv()
                heads = half_of(g, d)
                part[k, heads, s] = (
                    part[k, heads, s].astype(F32) + core_in[heads, s].astype(F32)
                    + xhalf[place[d], g, :, zslot(dz)].astype(F32)
                ).astype(BF16)
                full_in[g, dz, d] = send(
                    part.at[k, groups[g], s], xfull.at[place[d], groups[g], zslot(dz)], xs[d]
                )

    addends(0)
    x_arrivals(1)
    x_arrivals(-1)
    send_halves(0)
    addends(1)
    send_halves(1)

    x_arrivals(2)
    send_fulls(0)
    for copy in x_second[:6]:
        copy.wait_recv()
    for dz in (0, 1, -1):
        core_values.append(share(line(dx=2, dz=dz), sibling))
    send_fulls(1)

    for copy in x_second[6:]:
        copy.wait_recv()
    core_values.append(share(line(dx=2, dz=2), sibling))
    for copy in core_values:
        copy.wait_recv()
    table = jnp.zeros((128, 128), F32)
    for h in range(HEADS):
        weight_grad = lax.dot_general(
            ogs[:, h].reshape(128, 256), vals[:, h].reshape(512, 256),
            (((1,), (1,)), ((), ())), preferred_element_type=F32,
        )
        wgs[h] = weight_grad
        table = jnp.where(lanes == h, jnp.sum(weight_grad * wts[h], axis=1, keepdims=True), table)
    dots[col] = table.T[:8]
    dot_in = [send(dots.at[col], dots.at[col], device) for device in cols]

    def arrived(g, dz):
        s, heads = slot(0, dz), groups[g]
        total = part[k, heads, s].astype(F32) + core_in[heads, s].astype(F32)
        for d in (1, -1):
            full_in[g, dz, d].wait_recv()
            total += xfull[place[d], heads, zslot(dz)].astype(F32)
        return s, total

    z_full = {}
    for g, heads in enumerate(groups):
        for dz in (2, 1, -1):
            s, total = arrived(g, dz)
            part[k, heads, s] = total.astype(BF16)
            z_full[g, dz] = send(part.at[k, heads, s], zfull.at[place[dz], heads], zs[dz])

    for copy in dot_in:
        copy.wait_recv()
    row_dot = jnp.sum(dots[...], axis=0)
    row_dot = jnp.concatenate([row_dot] * 16, axis=0).T
    for h in range(HEADS):
        logit_grad_ref[h] = wts[h] * (wgs[h] - row_dot[:, h : h + 1])

    totals = []
    for g, heads in enumerate(groups):
        s, total = arrived(g, 0)
        for dz in (2, 1, -1):
            z_full[g, dz].wait_recv()
            total += zfull[place[dz], heads].astype(F32)
        totals += [total[h] for h in range(GROUP)]
    for s, piece in enumerate(regroup(totals, 32)):
        value_grad_ref[s] = piece.astype(BF16)

    for copy in started:
        copy.wait_send()


def store(logit_grad, value_grad, logit_grad_ref, value_grad_ref, sem):
    copies = [
        pltpu.make_async_copy(logit_grad, logit_grad_ref, sem.at[0]),
        pltpu.make_async_copy(value_grad, value_grad_ref, sem.at[1]),
    ]
    for copy in copies:
        copy.start()
    for copy in copies:
        copy.wait()


def per_device(logits, values, output_gradient):
    vmem = pl.BlockSpec(memory_space=pltpu.VMEM)
    hbm = pl.BlockSpec(memory_space=pltpu.HBM)
    copies = 136
    outs = (jax.ShapeDtypeStruct(logits.shape, F32), jax.ShapeDtypeStruct(values.shape, BF16))
    results = pl.pallas_call(
        kernel,
        out_shape=outs,
        in_specs=[hbm] * 3,
        out_specs=(vmem, vmem),
        scratch_shapes=[
            pltpu.VMEM((2, 8, BLOCK, 256), BF16),
            pltpu.VMEM((32, HEADS, BLOCK, 256), BF16),
            pltpu.VMEM((8, HEADS, BLOCK, 256), BF16),
            pltpu.VMEM((HEADS, BLOCK, 256), BF16),
            pltpu.VMEM((HEADS, 128, 512), F32),
            pltpu.VMEM((HEADS, 128, 512), F32),
            pltpu.VMEM((2, HEADS, 16, BLOCK, 256), BF16),
            pltpu.VMEM((HEADS, 16, BLOCK, 256), BF16),
            pltpu.VMEM((2, HEADS // GROUP, HALF, RING, BLOCK, 256), BF16),
            pltpu.VMEM((2, HEADS, RING, BLOCK, 256), BF16),
            pltpu.VMEM((3, HEADS, BLOCK, 256), BF16),
            pltpu.VMEM((8, 16, 128), F32),
            pltpu.VMEM((8, 8, 128), F32),
            pltpu.SemaphoreType.DMA((HEADS + 2,)),
            pltpu.SemaphoreType.DMA((copies,)),
            pltpu.SemaphoreType.DMA((copies,)),
        ],
        compiler_params=pltpu.CompilerParams(
            collective_id=0, has_side_effects=True, vmem_limit_bytes=52224 * 1024
        ),
    )(logits, values, output_gradient)
    return pl.pallas_call(
        store,
        out_shape=outs,
        in_specs=[pl.BlockSpec(memory_space=pl.ANY)] * 2,
        out_specs=(hbm, hbm),
        scratch_shapes=[pltpu.SemaphoreType.DMA((2,))],
        compiler_params=pltpu.CompilerParams(vmem_limit_bytes=1024 * 1024),
    )(*results)


def solution(mesh):
    placed = (P(None, "row", "col"), P(None, ("col", "row"), None), P(None, ("col", "row"), None))
    return jax.shard_map(
        per_device,
        mesh=mesh,
        in_specs=placed,
        out_specs=(P(None, "row", "col"), P(None, ("col", "row"), None)),
        check_vma=False,
    )
```

time: 58.9 us -> 50.6 us (0.86)
  Pallas kernels: 52.9 us -> 48.1 us
  local copies, waits for them, and re-layouts: 5.21 us -> 1.67 us
    pallas_call x1 -> x2, Pallas kernels: 52.9 us -> 48.1 us  [the longest x1 46.8 us: per_device(): pl.pallas_call(kernel, out_shape=outs, in_specs=[hbm] * 3, out_specs=(vme...]
    unnamed x8 -> x4, local copies, waits for them, and re-layouts: 5.21 us -> 1.67 us
where the time goes in v2:
time: 50.6 us; the launch traced here: 50.4 us
  Pallas kernels  48.1 us (95%)
  local copies, waits for them, and re-layouts  1.67 us (3%)
  between operations  0.65 us (1%)
    pallas_call x1, Pallas kernels, per_device(): pl.pallas_call(kernel, out_shape=outs, in_specs=[hbm] * 3, out_specs=(vme...  46.8 us
    unnamed x4, local copies, waits for them, and re-layouts  1.67 us
    pallas_call x1, Pallas kernels, per_device(): pl.pallas_call(store, out_shape=outs, in_specs=[pl.BlockSpec(memory_space...  1.34 us

profile of v2, /device:TPU:1, one launch (start us, length us, event | category | flops | bytes accessed | tf_op | source)
XLA Modules:
  0.0 50.4 jit_solution(13244662017387955080)
XLA Ops:
  0.6 0.0 copy-start
  0.6 0.8 %copy-done = bf16[8,16,256]{2,1,0:T(8,128)(2,1)S(1)} copy-done((bf16[8,16,256]{2,1,0:T(8,128)(2,1)S(1)}, bf16[8,16,256]{2,1,0:T(8,128)(2,1)}, u32[]{:S(2)}) %copy-start) | copy-done | bytes 65560
  1.5 0.0 copy-start.1
  1.5 0.8 %copy-done.1 = bf16[8,16,256]{2,1,0:T(8,128)(2,1)S(1)} copy-done((bf16[8,16,256]{2,1,0:T(8,128)(2,1)S(1)}, bf16[8,16,256]{2,1,0:T(8,128)(2,1)}, u32[]{:S(2)}) %copy-start.1) | copy-done | bytes 65560
  2.3 46.8 %shard_map.50 = (f32[8,128,512]{2,1,0:T(8,128)S(1)}, bf16[8,16,256]{2,1,0:T(8,128)(2,1)S(1)}) custom-call(f32[8,128,512]{2,1,0:T(8,128)} %logits_ref.1, bf16[8,16,256]{2,1,0:T(8,128)(2,1)S(1)} %copy-done, bf16[8,16,256]{2,1,0:T(8,128)(2,1)S(1)} %copy-done.1), custom_call_target="tpu_custom_call" | custom-call | tf_op jit(solution)/shard_map/pallas_call | solution.py:302
  49.1 1.3 %shard_map.51 = (f32[8,128,512]{2,1,0:T(8,128)}, bf16[8,16,256]{2,1,0:T(8,128)(2,1)}) custom-call(f32[8,128,512]{2,1,0:T(8,128)S(1)} %get-tuple-element.4.logit_grad, bf16[8,16,256]{2,1,0:T(8,128)(2,1)S(1)} %get-tuple-element.5.value_grad), custom_call_target="tpu_custom_call" | custom-call | tf_op jit(solution)/shard_map/pallas_call | solution.py:329
Async XLA Ops:
  0.6 0.8 %copy-start = (bf16[8,16,256]{2,1,0:T(8,128)(2,1)S(1)}, bf16[8,16,256]{2,1,0:T(8,128)(2,1)}, u32[]{:S(2)}) copy-start(bf16[8,16,256]{2,1,0:T(8,128)(2,1)} %values_ref.1) | copy-start | bytes 196612
  1.5 0.8 %copy-start.1 = (bf16[8,16,256]{2,1,0:T(8,128)(2,1)S(1)}, bf16[8,16,256]{2,1,0:T(8,128)(2,1)}, u32[]{:S(2)}) copy-start(bf16[8,16,256]{2,1,0:T(8,128)(2,1)} %grads_ref.1) | copy-start | bytes 196612

commit v3 on v2

--- a/solution.py
+++ b/solution.py
@@ -39,8 +39,8 @@
     def slot(dx=0, dz=0):
         return (x + dx + 4) % 4 * 4 + (zh + dz + 4) % 4
 
-    def line(dx=0, dz=0, core=k):
-        return slot(dx, dz) * 2 + core
+    def slots(dx):
+        return pl.ds((x + dx + 4) % 4 * 4, 4)
 
     started = []
 
@@ -83,7 +83,7 @@
         own_grads[h] = piece
     loads[1].wait()
     for h, piece in enumerate(regroup([raw[1, s] for s in range(8)], 32)):
-        vals[row, h] = piece
+        vals[slot(), k, h] = piece
     loads = loads[2:]
 
     pl.semaphore_wait(barrier, len(greeted))
@@ -94,24 +94,31 @@
     grads_in = [send(own_grads.at[heads], ogs.at[piece, heads], grads_to) for heads in groups]
 
     def share(ref_slot, where, heads=None):
-        ref = vals.at[ref_slot] if heads is None else vals.at[ref_slot, pl.ds(heads, 4)]
+        ref = vals.at[ref_slot, k] if heads is None else vals.at[ref_slot, k, pl.ds(heads, 4)]
         return send(ref, ref, where)
 
-    x_first = {0: {d: share(row, xs[d]) for d in (1, -1)}}
-    z_first = {d: share(row, zs[d]) for d in (1, -1)}
+    x_first = {0: {d: share(slot(), xs[d]) for d in (1, -1)}}
+    z_first = {d: share(slot(), zs[d]) for d in (1, -1)}
     z_second = {}
-    core_values = [share(row, sibling)]
+    core_values = []
 
     lanes = lax.broadcasted_iota(jnp.int32, (128, 128), 1)
     table = jnp.zeros((128, 128), F32)
-    for h in range(HEADS):
-        loads[h].wait()
+
+    def column(wide, h):
+        return jnp.sum(jnp.where(lanes == h, wide, 0.0), axis=1, keepdims=True)
+
+    def head_stats(h, table):
         block = wts[h]
         top = jnp.max(block, axis=1, keepdims=True)
         exponent = jnp.exp(block - top)
         wts[h] = exponent
         table = jnp.where(lanes == h, top, table)
-        table = jnp.where(lanes == 8 + h, jnp.sum(exponent, axis=1, keepdims=True), table)
+        return jnp.where(lanes == 8 + h, jnp.sum(exponent, axis=1, keepdims=True), table)
+
+    for load in loads:
+        load.wait()
+    table = lax.fori_loop(0, HEADS, head_stats, table)
     stat[col] = table.T[:16]
     stat_in = [send(stat.at[col], stat.at[col], device) for device in cols]
 
@@ -127,7 +134,7 @@
         y_in.append([pass_on(mine, heads, ys[d]) for d in (1, -1, 2)])
 
     def z_arrival(d):
-        got = line(dz=-d)
+        got = slot(dz=-d)
         if d == 2:
             for copy in z_second.values():
                 copy.wait_recv()
@@ -135,16 +142,17 @@
             z_first[d].wait_recv()
             z_second[d] = share(got, zs[d], 0 if d == 1 else 4)
         x_first[2 if d == 2 else -d] = {e: share(got, xs[e]) for e in (1, -1)}
-        core_values.append(share(got, sibling))
 
     x_second = []
 
+    def share_core(dx):
+        core_values.append(send(vals.at[slots(dx), k], vals.at[slots(dx), k], sibling))
+
     def x_arrivals(dz):
         for d in (1, -1):
             x_first[dz][d].wait_recv()
-            got = line(dx=-d, dz=dz)
+            got = slot(dx=-d, dz=dz)
             x_second.append(share(got, xs[d], 0 if d == 1 else 4))
-            core_values.append(share(got, sibling))
 
     z_arrival(1)
     z_arrival(-1)
@@ -160,25 +168,33 @@
     total = jnp.sum(sums * jnp.exp(tops - top[None]), axis=0)
     factor = jnp.exp(stat[col, 0:8, :] - top) / total
     factor = jnp.concatenate([factor] * 16, axis=0).T
-    for h in range(HEADS):
-        wts[h] = wts[h] * factor[:, h : h + 1]
+
+    def scale(h, carry):
+        wts[h] = wts[h] * column(factor, h)
+        return carry
+
+    lax.fori_loop(0, HEADS, scale, 0)
     z_arrival(2)
+    share_core(0)
 
     core_sums = []
+
+    def addend_of(h, carry):
+        og = ogs[:, h].reshape(128, 256)
+        addend = lax.dot_general(
+            wts[h].astype(BF16), og, (((0,), (0,)), ((), ())), preferred_element_type=F32
+        ).astype(BF16).reshape(16, 2, BLOCK, 256)
+        part[0, h] = addend[:, 0]
+        part[1, h] = addend[:, 1]
+        return carry
 
     def addends(g):
         for copy in y_in[g]:
             copy.wait_recv()
-        for h in range(g * GROUP, (g + 1) * GROUP):
-            og = ogs[:, h].reshape(128, 256)
-            addend = lax.dot_general(
-                wts[h].astype(BF16), og, (((0,), (0,)), ((), ())), preferred_element_type=F32
-            ).astype(BF16).reshape(16, 2, BLOCK, 256)
-            part[0, h] = addend[:, 0]
-            part[1, h] = addend[:, 1]
-            if h % HALF == HALF - 1:
-                heads = pl.ds(h - HALF + 1, HALF)
-                core_sums.append(send(part.at[1 - k, heads], core_in.at[heads], sibling))
+        for start in range(g * GROUP, (g + 1) * GROUP, HALF):
+            lax.fori_loop(start, start + HALF, addend_of, 0)
+            heads = pl.ds(start, HALF)
+            core_sums.append(send(part.at[1 - k, heads], core_in.at[heads], sibling))
 
     order = (2, 1, -1, 0)
     place = {1: 0, -1: 1, 2: 2}
@@ -193,59 +209,30 @@
 
     def send_halves(g):
         for d in (1, -1):
-            heads = half_of(g, d)
+            heads, there = half_of(g, d), slots(2)
             core_sums[g * 2 + place[d]].wait_recv()
+            part[k, heads, there] = (
+                part[k, heads, there].astype(F32) + core_in[heads, there].astype(F32)
+            ).astype(BF16)
+            half_in[g, d] = send(part.at[k, heads, there], xhalf.at[place[d], g], xs[d])
+
+    def send_fulls(g):
+        for d in (1, -1):
+            heads, there = half_of(g, -d), slots(d)
+            part[k, heads, there] = (
+                part[k, heads, there].astype(F32) + core_in[heads, there].astype(F32)
+            ).astype(BF16)
+        for d in (1, -1):
+            heads, there = half_of(g, d), slots(d)
+            half_in[g, d].wait_recv()
+            part[k, heads, there] = (
+                part[k, heads, there].astype(F32) + core_in[heads, there].astype(F32)
+                + xhalf[place[d], g].astype(F32)
+            ).astype(BF16)
             for dz in order:
-                s = slot(2, dz)
-                part[k, heads, s] = (part[k, heads, s].astype(F32) + core_in[heads, s].astype(F32)).astype(BF16)
-                half_in[g, dz, d] = send(part.at[k, heads, s], xhalf.at[place[d], g, :, zslot(dz)], xs[d])
-
-    def send_fulls(g):
-        for dz in order:
-            for d in (1, -1):
-                s = slot(d, dz)
-                heads = half_of(g, -d)
-                part[k, heads, s] = (part[k, heads, s].astype(F32) + core_in[heads, s].astype(F32)).astype(BF16)
-                half_in[g, dz, d].wait_recv()
-                heads = half_of(g, d)
-                part[k, heads, s] = (
-                    part[k, heads, s].astype(F32) + core_in[heads, s].astype(F32)
-                    + xhalf[place[d], g, :, zslot(dz)].astype(F32)
-                ).astype(BF16)
                 full_in[g, dz, d] = send(
-                    part.at[k, groups[g], s], xfull.at[place[d], groups[g], zslot(dz)], xs[d]
+                    part.at[k, groups[g], slot(d, dz)], xfull.at[place[d], groups[g], zslot(dz)], xs[d]
                 )
-
-    addends(0)
-    x_arrivals(1)
-    x_arrivals(-1)
-    send_halves(0)
-    addends(1)
-    send_halves(1)
-
-    x_arrivals(2)
-    send_fulls(0)
-    for copy in x_second[:6]:
-        copy.wait_recv()
-    for dz in (0, 1, -1):
-        core_values.append(share(line(dx=2, dz=dz), sibling))
-    send_fulls(1)
-
-    for copy in x_second[6:]:
-        copy.wait_recv()
-    core_values.append(share(line(dx=2, dz=2), sibling))
-    for copy in core_values:
-        copy.wait_recv()
-    table = jnp.zeros((128, 128), F32)
-    for h in range(HEADS):
-        weight_grad = lax.dot_general(
-            ogs[:, h].reshape(128, 256), vals[:, h].reshape(512, 256),
-            (((1,), (1,)), ((), ())), preferred_element_type=F32,
-        )
-        wgs[h] = weight_grad
-        table = jnp.where(lanes == h, jnp.sum(weight_grad * wts[h], axis=1, keepdims=True), table)
-    dots[col] = table.T[:8]
-    dot_in = [send(dots.at[col], dots.at[col], device) for device in cols]
 
     def arrived(g, dz):
         s, heads = slot(0, dz), groups[g]
@@ -256,16 +243,55 @@
         return s, total
 
     z_full = {}
-    for g, heads in enumerate(groups):
+
+    def send_on(g):
+        heads = groups[g]
         for dz in (2, 1, -1):
             s, total = arrived(g, dz)
             part[k, heads, s] = total.astype(BF16)
             z_full[g, dz] = send(part.at[k, heads, s], zfull.at[place[dz], heads], zs[dz])
 
+    x_arrivals(1)
+    x_arrivals(-1)
+    addends(0)
+    send_halves(0)
+    addends(1)
+    send_halves(1)
+
+    x_arrivals(2)
+    share_core(1)
+    share_core(-1)
+    send_fulls(0)
+    send_fulls(1)
+    send_on(0)
+
+    for copy in x_second:
+        copy.wait_recv()
+    share_core(2)
+    for copy in core_values:
+        copy.wait_recv()
+    table = jnp.zeros((128, 128), F32)
+
+    def weight_grads(h, table):
+        weight_grad = lax.dot_general(
+            ogs[:, h].reshape(128, 256), vals[:, :, h].reshape(512, 256),
+            (((1,), (1,)), ((), ())), preferred_element_type=F32,
+        )
+        wgs[h] = weight_grad
+        return jnp.where(lanes == h, jnp.sum(weight_grad * wts[h], axis=1, keepdims=True), table)
+
+    for h in range(HEADS):
+        table = weight_grads(h, table)
+    dots[col] = table.T[:8]
+    dot_in = [send(dots.at[col], dots.at[col], device) for device in cols]
+
+    send_on(1)
+
     for copy in dot_in:
         copy.wait_recv()
     row_dot = jnp.sum(dots[...], axis=0)
     row_dot = jnp.concatenate([row_dot] * 16, axis=0).T
+
     for h in range(HEADS):
         logit_grad_ref[h] = wts[h] * (wgs[h] - row_dot[:, h : h + 1])
 
@@ -306,7 +332,7 @@
         out_specs=(vmem, vmem),
         scratch_shapes=[
             pltpu.VMEM((2, 8, BLOCK, 256), BF16),
-            pltpu.VMEM((32, HEADS, BLOCK, 256), BF16),
+            pltpu.VMEM((16, 2, HEADS, BLOCK, 256), BF16),
             pltpu.VMEM((8, HEADS, BLOCK, 256), BF16),
             pltpu.VMEM((HEADS, BLOCK, 256), BF16),
             pltpu.VMEM((HEADS, 128, 512), F32),
@@ -323,9 +349,9 @@
             pltpu.SemaphoreType.DMA((copies,)),
         ],
         compiler_params=pltpu.CompilerParams(
-            collective_id=0, has_side_effects=True, vmem_limit_bytes=52224 * 1024
+            collective_id=0, has_side_effects=True, vmem_limit_bytes=40 * 1024 * 1024
         ),
-    )(logits, values, output_gradient)
+    )(*(pltpu.with_memory_space_constraint(a, pltpu.HBM) for a in (logits, values, output_gradient)))
     return pl.pallas_call(
         store,
         out_shape=outs,

time: 50.6 us -> 49 us (0.968)
  local copies, waits for them, and re-layouts: 1.67 us -> 0 us
    unnamed x4 -> x0, local copies, waits for them, and re-layouts: 1.67 us -> none
where the time goes in v3:
time: 49 us; the launch traced here: 48.9 us
  Pallas kernels  48.2 us (98%)
  between operations  0.64 us (1%)
    pallas_call x1, Pallas kernels, per_device(): pl.pallas_call(kernel, out_shape=outs, in_specs=[hbm] * 3, out_specs=(vme...  46.9 us
    pallas_call x1, Pallas kernels, per_device(): pl.pallas_call(store, out_shape=outs, in_specs=[pl.BlockSpec(memory_space...  1.34 us

profile of v3, /device:TPU:1, one launch (start us, length us, event | category | flops | bytes accessed | tf_op | source)
XLA Modules:
  0.0 48.9 jit_solution(9465362647082552088)
XLA Ops:
  0.6 46.9 %shard_map.50 = (f32[8,128,512]{2,1,0:T(8,128)S(1)}, bf16[8,16,256]{2,1,0:T(8,128)(2,1)S(1)}) custom-call(f32[8,128,512]{2,1,0:T(8,128)} %logits_ref.1, bf16[8,16,256]{2,1,0:T(8,128)(2,1)} %values_ref.1, bf16[8,16,256]{2,1,0:T(8,128)(2,1)} %grads_ref.1), custom_call_target="tpu_custom_call" | custom-call | tf_op jit(solution)/shard_map/pallas_call | solution.py:328
  47.5 1.3 %shard_map.51 = (f32[8,128,512]{2,1,0:T(8,128)}, bf16[8,16,256]{2,1,0:T(8,128)(2,1)}) custom-call(f32[8,128,512]{2,1,0:T(8,128)S(1)} %get-tuple-element.4.logit_grad, bf16[8,16,256]{2,1,0:T(8,128)(2,1)S(1)} %get-tuple-element.5.value_grad), custom_call_target="tpu_custom_call" | custom-call | tf_op jit(solution)/shard_map/pallas_call | solution.py:355

commit v4 on v3

--- a/solution.py
+++ b/solution.py
@@ -10,7 +10,6 @@
 RING = 4
 HEADS = 8
 GROUP = 4
-HALF = 2
 BLOCK = 16
 F32 = jnp.float32
 BF16 = jnp.bfloat16
@@ -26,7 +25,7 @@
 
 def kernel(
     logits_ref, values_ref, grads_ref, logit_grad_ref, value_grad_ref,
-    raw, vals, ogs, own_grads, wts, wgs, part, core_in, xhalf, xfull, zfull,
+    raw, vals, ogs, own_grads, wts, wgs, part, core_in, xhalf, xfull, zfull, zearly, early_sum, xlate,
     stat, dots, load_sem, send_sem, recv_sem,
 ):
     row, col = lax.axis_index("row"), lax.axis_index("col")
@@ -55,7 +54,7 @@
         return copy
 
     sibling = at(k=1 - k)
-    xs = {d: at(x=x + d + 4) for d in (1, -1)}
+    xs = {d: at(x=x + d + 4) for d in (1, -1, 2)}
     zs = {d: at(zh=zh + d + 4) for d in (1, -1, 2)}
     ys = {d: at(y=y + d + 4) for d in (1, -1, 2)}
     twin = at(zl=1 - zl)
@@ -177,93 +176,135 @@
     z_arrival(2)
     share_core(0)
 
-    core_sums = []
 
     def addend_of(h, carry):
         og = ogs[:, h].reshape(128, 256)
         addend = lax.dot_general(
             wts[h].astype(BF16), og, (((0,), (0,)), ((), ())), preferred_element_type=F32
-        ).astype(BF16).reshape(16, 2, BLOCK, 256)
-        part[0, h] = addend[:, 0]
-        part[1, h] = addend[:, 1]
+        ).astype(BF16).reshape(4, 4, 2, BLOCK, 256)
+        part[0, h] = addend[:, :, 0]
+        part[1, h] = addend[:, :, 1]
         return carry
 
-    def addends(g):
-        for copy in y_in[g]:
-            copy.wait_recv()
-        for start in range(g * GROUP, (g + 1) * GROUP, HALF):
-            lax.fori_loop(start, start + HALF, addend_of, 0)
-            heads = pl.ds(start, HALF)
-            core_sums.append(send(part.at[1 - k, heads], core_in.at[heads], sibling))
+    core_sums = {}
+
+    def addends(start, count):
+        lax.fori_loop(start, start + count, addend_of, 0)
+        heads = pl.ds(start, count)
+        core_sums[start] = send(part.at[1 - k, heads], core_in.at[heads], sibling)
 
     order = (2, 1, -1, 0)
     place = {1: 0, -1: 1, 2: 2}
-
-    def half_of(g, d):
-        return pl.ds(g * GROUP + (0 if d == 1 else HALF), HALF)
+    first, second = (2, 1), (4, 2)
+
+    def heads_of(group):
+        return pl.ds(group[0], 2 * group[1])
+
+    def half_of(group, d):
+        return pl.ds(group[0] + (0 if d == 1 else group[1]), group[1])
+
+    def held(group, d):
+        return xhalf.at[place[d], pl.ds(group[0] // 2, group[1])]
+
+    def plane(dx):
+        return (x + dx + 4) % 4
 
     def zslot(dz):
         return (zh + dz + 4) % 4
 
     half_in, full_in = {}, {}
 
-    def send_halves(g):
+    def send_halves(group):
         for d in (1, -1):
-            heads, there = half_of(g, d), slots(2)
-            core_sums[g * 2 + place[d]].wait_recv()
+            heads, there = half_of(group, d), plane(2)
+            core_sums[half_start(group, d)].wait_recv()
             part[k, heads, there] = (
                 part[k, heads, there].astype(F32) + core_in[heads, there].astype(F32)
             ).astype(BF16)
-            half_in[g, d] = send(part.at[k, heads, there], xhalf.at[place[d], g], xs[d])
-
-    def send_fulls(g):
+            half_in[group, d] = send(part.at[k, heads, there], held(group, d), xs[d])
+
+    def half_start(group, d):
+        return group[0] + (0 if d == 1 else group[1])
+
+    def send_fulls(group):
         for d in (1, -1):
-            heads, there = half_of(g, -d), slots(d)
+            heads, there = half_of(group, -d), plane(d)
             part[k, heads, there] = (
                 part[k, heads, there].astype(F32) + core_in[heads, there].astype(F32)
             ).astype(BF16)
         for d in (1, -1):
-            heads, there = half_of(g, d), slots(d)
-            half_in[g, d].wait_recv()
+            heads, there = half_of(group, d), plane(d)
+            half_in[group, d].wait_recv()
             part[k, heads, there] = (
                 part[k, heads, there].astype(F32) + core_in[heads, there].astype(F32)
-                + xhalf[place[d], g].astype(F32)
+                + held(group, d)[...].astype(F32)
             ).astype(BF16)
             for dz in order:
-                full_in[g, dz, d] = send(
-                    part.at[k, groups[g], slot(d, dz)], xfull.at[place[d], groups[g], zslot(dz)], xs[d]
+                full_in[group, dz, d] = send(
+                    part.at[k, heads_of(group), there, zslot(dz)],
+                    xfull.at[place[d], heads_of(group), zslot(dz)], xs[d],
                 )
 
-    def arrived(g, dz):
-        s, heads = slot(0, dz), groups[g]
-        total = part[k, heads, s].astype(F32) + core_in[heads, s].astype(F32)
+    def arrived(group, dz):
+        heads, here = heads_of(group), zslot(dz)
+        total = part[k, heads, x, here].astype(F32) + core_in[heads, x, here].astype(F32)
         for d in (1, -1):
-            full_in[g, dz, d].wait_recv()
-            total += xfull[place[d], heads, zslot(dz)].astype(F32)
-        return s, total
+            full_in[group, dz, d].wait_recv()
+            total += xfull[place[d], heads, here].astype(F32)
+        return total
 
     z_full = {}
 
-    def send_on(g):
-        heads = groups[g]
+    def send_on(group):
+        heads = heads_of(group)
         for dz in (2, 1, -1):
-            s, total = arrived(g, dz)
-            part[k, heads, s] = total.astype(BF16)
-            z_full[g, dz] = send(part.at[k, heads, s], zfull.at[place[dz], heads], zs[dz])
+            here = zslot(dz)
+            part[k, heads, x, here] = arrived(group, dz).astype(BF16)
+            z_full[group, dz] = send(part.at[k, heads, x, here], zfull.at[place[dz], heads], zs[dz])
+
+    z_early, x_late = {}, {}
+
+    def send_early():
+        heads = pl.ds(0, 2)
+        core_sums[0].wait_recv()
+        for dz in (2, 1, -1):
+            here = zslot(dz)
+            part[k, heads, :, here] = (
+                part[k, heads, :, here].astype(F32) + core_in[heads, :, here].astype(F32)
+            ).astype(BF16)
+            z_early[dz] = send(part.at[k, heads, :, here], zearly.at[place[dz]], zs[dz])
+
+    def send_late():
+        heads = pl.ds(0, 2)
+        total = part[k, heads, :, zh].astype(F32) + core_in[heads, :, zh].astype(F32)
+        for dz in (2, 1, -1):
+            z_early[dz].wait_recv()
+            total += zearly[place[dz]].astype(F32)
+        early_sum[...] = total.astype(BF16)
+        for dx in (2, 1, -1):
+            x_late[dx] = send(early_sum.at[:, plane(dx)], xlate.at[place[dx]], xs[dx])
 
     x_arrivals(1)
     x_arrivals(-1)
-    addends(0)
-    send_halves(0)
-    addends(1)
-    send_halves(1)
+    for copy in y_in[0]:
+        copy.wait_recv()
+    addends(2, 1)
+    addends(3, 1)
+    addends(0, 2)
+    send_halves(first)
+    send_early()
+    for copy in y_in[1]:
+        copy.wait_recv()
+    addends(4, 2)
+    addends(6, 2)
+    send_halves(second)
 
     x_arrivals(2)
     share_core(1)
     share_core(-1)
-    send_fulls(0)
-    send_fulls(1)
-    send_on(0)
+    send_fulls(first)
+    send_fulls(second)
+    send_on(first)
 
     for copy in x_second:
         copy.wait_recv()
@@ -284,8 +325,9 @@
         table = weight_grads(h, table)
     dots[col] = table.T[:8]
     dot_in = [send(dots.at[col], dots.at[col], device) for device in cols]
-
-    send_on(1)
+    send_late()
+
+    send_on(second)
 
     for copy in dot_in:
         copy.wait_recv()
@@ -295,13 +337,17 @@
     for h in range(HEADS):
         logit_grad_ref[h] = wts[h] * (wgs[h] - row_dot[:, h : h + 1])
 
-    totals = []
-    for g, heads in enumerate(groups):
-        s, total = arrived(g, 0)
+    early = early_sum[:, x].astype(F32)
+    for dx in (2, 1, -1):
+        x_late[dx].wait_recv()
+        early += xlate[place[dx]].astype(F32)
+    totals = [early[0], early[1]]
+    for group in (first, second):
+        total = arrived(group, 0)
         for dz in (2, 1, -1):
-            z_full[g, dz].wait_recv()
-            total += zfull[place[dz], heads].astype(F32)
-        totals += [total[h] for h in range(GROUP)]
+            z_full[group, dz].wait_recv()
+            total += zfull[place[dz], heads_of(group)].astype(F32)
+        totals += [total[h] for h in range(2 * group[1])]
     for s, piece in enumerate(regroup(totals, 32)):
         value_grad_ref[s] = piece.astype(BF16)
 
@@ -337,11 +383,14 @@
             pltpu.VMEM((HEADS, BLOCK, 256), BF16),
             pltpu.VMEM((HEADS, 128, 512), F32),
             pltpu.VMEM((HEADS, 128, 512), F32),
-            pltpu.VMEM((2, HEADS, 16, BLOCK, 256), BF16),
-            pltpu.VMEM((HEADS, 16, BLOCK, 256), BF16),
-            pltpu.VMEM((2, HEADS // GROUP, HALF, RING, BLOCK, 256), BF16),
+            pltpu.VMEM((2, HEADS, RING, RING, BLOCK, 256), BF16),
+            pltpu.VMEM((HEADS, RING, RING, BLOCK, 256), BF16),
+            pltpu.VMEM((2, 4, RING, BLOCK, 256), BF16),
             pltpu.VMEM((2, HEADS, RING, BLOCK, 256), BF16),
             pltpu.VMEM((3, HEADS, BLOCK, 256), BF16),
+            pltpu.VMEM((3, 2, RING, BLOCK, 256), BF16),
+            pltpu.VMEM((2, RING, BLOCK, 256), BF16),
+            pltpu.VMEM((3, 2, BLOCK, 256), BF16),
             pltpu.VMEM((8, 16, 128), F32),
             pltpu.VMEM((8, 8, 128), F32),
             pltpu.SemaphoreType.DMA((HEADS + 2,)),

time: 49 us -> 48.1 us (0.982)
  Pallas kernels: 48.2 us -> 47.3 us
    pallas_call x1, Pallas kernels: 46.9 us -> 46 us  [per_device(): pl.pallas_call(kernel, out_shape=outs, in_specs=[hbm] * 3, out_specs=(vme...]
where the time goes in v4:
time: 48.1 us; the launch traced here: 48 us
  Pallas kernels  47.3 us (98%)
  between operations  0.64 us (1%)
    pallas_call x1, Pallas kernels, per_device(): pl.pallas_call(kernel, out_shape=outs, in_specs=[hbm] * 3, out_specs=(vme...  46 us
    pallas_call x1, Pallas kernels, per_device(): pl.pallas_call(store, out_shape=outs, in_specs=[pl.BlockSpec(memory_space...  1.34 us

profile of v4, /device:TPU:1, one launch (start us, length us, event | category | flops | bytes accessed | tf_op | source)
XLA Modules:
  0.0 48.0 jit_solution(8166208252092233443)
XLA Ops:
  0.6 46.0 %shard_map.50 = (f32[8,128,512]{2,1,0:T(8,128)S(1)}, bf16[8,16,256]{2,1,0:T(8,128)(2,1)S(1)}) custom-call(f32[8,128,512]{2,1,0:T(8,128)} %logits_ref.1, bf16[8,16,256]{2,1,0:T(8,128)(2,1)} %values_ref.1, bf16[8,16,256]{2,1,0:T(8,128)(2,1)} %grads_ref.1), custom_call_target="tpu_custom_call" | custom-call | tf_op jit(solution)/shard_map/pallas_call | solution.py:374
  46.6 1.3 %shard_map.51 = (f32[8,128,512]{2,1,0:T(8,128)}, bf16[8,16,256]{2,1,0:T(8,128)(2,1)}) custom-call(f32[8,128,512]{2,1,0:T(8,128)S(1)} %get-tuple-element.4.logit_grad, bf16[8,16,256]{2,1,0:T(8,128)(2,1)S(1)} %get-tuple-element.5.value_grad), custom_call_target="tpu_custom_call" | custom-call | tf_op jit(solution)/shard_map/pallas_call | solution.py:404

commit v5 on v4

--- a/solution.py
+++ b/solution.py
@@ -189,7 +189,7 @@
     core_sums = {}
 
     def addends(start, count):
-        lax.fori_loop(start, start + count, addend_of, 0)
+        lax.fori_loop(start, start + count, addend_of, 0, unroll=True)
         heads = pl.ds(start, count)
         core_sums[start] = send(part.at[1 - k, heads], core_in.at[heads], sibling)
 
@@ -293,22 +293,22 @@
     addends(0, 2)
     send_halves(first)
     send_early()
+    x_arrivals(2)
+    share_core(1)
+    share_core(-1)
     for copy in y_in[1]:
         copy.wait_recv()
     addends(4, 2)
     addends(6, 2)
     send_halves(second)
 
-    x_arrivals(2)
-    share_core(1)
-    share_core(-1)
     send_fulls(first)
     send_fulls(second)
+    for copy in x_second:
+        copy.wait_recv()
+    share_core(2)
     send_on(first)
 
-    for copy in x_second:
-        copy.wait_recv()
-    share_core(2)
     for copy in core_values:
         copy.wait_recv()
     table = jnp.zeros((128, 128), F32)

time: 48.1 us -> 46.9 us (0.975); the launches traced: 48 us -> 46.2 us
  Pallas kernels: 47.3 us -> 45.6 us
    pallas_call x1, Pallas kernels: 46 us -> 44.3 us  [per_device(): pl.pallas_call(kernel, out_shape=outs, in_specs=[hbm] * 3, out_specs=(vme...]
where the time goes in v5:
time: 46.9 us; the launch traced here: 46.2 us
  Pallas kernels  45.6 us (97%)
  between operations  0.64 us (1%)
    pallas_call x1, Pallas kernels, per_device(): pl.pallas_call(kernel, out_shape=outs, in_specs=[hbm] * 3, out_specs=(vme...  44.3 us
    pallas_call x1, Pallas kernels, per_device(): pl.pallas_call(store, out_shape=outs, in_specs=[pl.BlockSpec(memory_space...  1.34 us

profile of v5, /device:TPU:1, one launch (start us, length us, event | category | flops | bytes accessed | tf_op | source)
XLA Modules:
  0.0 46.2 jit_solution(15600655526482380895)
XLA Ops:
  0.6 44.3 %shard_map.50 = (f32[8,128,512]{2,1,0:T(8,128)S(1)}, bf16[8,16,256]{2,1,0:T(8,128)(2,1)S(1)}) custom-call(f32[8,128,512]{2,1,0:T(8,128)} %logits_ref.1, bf16[8,16,256]{2,1,0:T(8,128)(2,1)} %values_ref.1, bf16[8,16,256]{2,1,0:T(8,128)(2,1)} %grads_ref.1), custom_call_target="tpu_custom_call" | custom-call | tf_op jit(solution)/shard_map/pallas_call | solution.py:374
  44.9 1.3 %shard_map.51 = (f32[8,128,512]{2,1,0:T(8,128)}, bf16[8,16,256]{2,1,0:T(8,128)(2,1)}) custom-call(f32[8,128,512]{2,1,0:T(8,128)S(1)} %get-tuple-element.4.logit_grad, bf16[8,16,256]{2,1,0:T(8,128)(2,1)S(1)} %get-tuple-element.5.value_grad), custom_call_target="tpu_custom_call" | custom-call | tf_op jit(solution)/shard_map/pallas_call | solution.py:404

commit v6 on v5

--- a/solution.py
+++ b/solution.py
@@ -303,10 +303,10 @@
     send_halves(second)
 
     send_fulls(first)
+    for copy in x_second:
+        copy.wait_recv()
+    share_core(2)
     send_fulls(second)
-    for copy in x_second:
-        copy.wait_recv()
-    share_core(2)
     send_on(first)
 
     for copy in core_values:

time: 46.9 us -> 46.7 us (level); the launches traced: 46.2 us -> 46.6 us
  no operation moved by 1% of the time
where the time goes in v6:
time: 46.7 us; the launch traced here: 46.6 us
  Pallas kernels  45.9 us (98%)
  between operations  0.64 us (1%)
    pallas_call x1, Pallas kernels, per_device(): pl.pallas_call(kernel, out_shape=outs, in_specs=[hbm] * 3, out_specs=(vme...  44.6 us
    pallas_call x1, Pallas kernels, per_device(): pl.pallas_call(store, out_shape=outs, in_specs=[pl.BlockSpec(memory_space...  1.34 us

profile of v6, /device:TPU:1, one launch (start us, length us, event | category | flops | bytes accessed | tf_op | source)
XLA Modules:
  0.0 46.6 jit_solution(15755144078705446971)
XLA Ops:
  0.6 44.6 %shard_map.50 = (f32[8,128,512]{2,1,0:T(8,128)S(1)}, bf16[8,16,256]{2,1,0:T(8,128)(2,1)S(1)}) custom-call(f32[8,128,512]{2,1,0:T(8,128)} %logits_ref.1, bf16[8,16,256]{2,1,0:T(8,128)(2,1)} %values_ref.1, bf16[8,16,256]{2,1,0:T(8,128)(2,1)} %grads_ref.1), custom_call_target="tpu_custom_call" | custom-call | tf_op jit(solution)/shard_map/pallas_call | solution.py:374
  45.2 1.3 %shard_map.51 = (f32[8,128,512]{2,1,0:T(8,128)}, bf16[8,16,256]{2,1,0:T(8,128)(2,1)}) custom-call(f32[8,128,512]{2,1,0:T(8,128)S(1)} %get-tuple-element.4.logit_grad, bf16[8,16,256]{2,1,0:T(8,128)(2,1)S(1)} %get-tuple-element.5.value_grad), custom_call_target="tpu_custom_call" | custom-call | tf_op jit(solution)/shard_map/pallas_call | solution.py:404
